TPU v7x, 32 devices: a whole 2x2x4 slice. The times are simulated.
32 devices in a mesh: groups: 2 (over x), chan: 16 (over z, y, core).
Axes of the slice: x: 2, y: 2, z: 4, core: 2. Of those that a mesh axis runs over, the one named last changes fastest.
Arguments:
- records: bfloat16 [256, 32, 2048], P(('groups', 'chan')), parts along dimension 0, may hold values from -6 to 6
- window_valid: float32 [256, 32], P(('groups', 'chan')), parts along dimension 0, may hold values from 0 to 1, as said below
- band_low: int32 [256], P(('groups', 'chan')), parts along dimension 0, may hold values from 0 to 255
- band_high: int32 [256], P(('groups', 'chan')), parts along dimension 0, may hold values from 768 to 1024
- pair_counts: int32 [32], P('groups'), parts along dimension 0, may hold values from 1 to 4, 32 in all
- partners: int32 [32, 4], P('groups'), parts along dimension 0, may hold values from 0 to 15
Outputs:
- stacks: bfloat16 [32, 4, 1024, 128], P(('groups', 'chan')), parts along dimension 0
There are 2 independent parts, one for each index of `groups`. A program takes and returns all parts, laid end to end along the dimension named above; each array names one. Nothing has to cross between parts.
Inputs may be any that keep to these rules, and one draw needn't show every extreme that they name: `window_valid`: 0 marks a window without data; some channels have no window with data. `pair_counts`: the counts sum to 32, and the largest is 4.
All inputs are finite; a program needn't handle non-finite values.
Results may differ from a plain program's by a relative error of at most 0.0065.
Values may be sent and summed in bfloat16 or wider, within the bound.
A program may use at most 128 MiB of HBM per device.

v0:
```python
import functools
import math

import jax
import jax.numpy as jnp
import ml_dtypes
import numpy as np
from jax import lax
from jax.experimental import pallas as pl
from jax.experimental.pallas import tpu as pltpu
from jax.sharding import PartitionSpec as P

SMOOTH = 8


def dft_table(length, first_bin, bin_count):
    sample_index = lax.broadcasted_iota(jnp.int32, (length, bin_count), 0)
    bin_index = lax.broadcasted_iota(jnp.int32, (length, bin_count), 1) + first_bin
    phase_step = sample_index * bin_index % length
    angles = phase_step.astype(jnp.float32) * (2.0 * math.pi / length)
    return jnp.concatenate([jnp.cos(angles), -jnp.sin(angles)], axis=1).astype(jnp.bfloat16)


def finish(spectrum, band_low, band_high, channels, windows):
    bin_total = spectrum.shape[1]
    magnitude = jnp.sqrt(spectrum[0] * spectrum[0] + spectrum[1] * spectrum[1])
    padded = jnp.pad(magnitude, ((SMOOTH, SMOOTH), (0, 0)))
    summed = padded[0:bin_total]
    for offset in range(1, 2 * SMOOTH + 1):
        summed = summed + padded[offset : offset + bin_total]
    bin_column = lax.broadcasted_iota(jnp.int32, (bin_total, 1), 0)
    in_range = (
        jnp.minimum(bin_column + SMOOTH, bin_total - 1) - jnp.maximum(bin_column - SMOOTH, 0) + 1
    )
    smoothed = summed / in_range.astype(jnp.float32)
    divisor = jnp.maximum(smoothed, 1.0).reshape(bin_total, channels, windows)
    bin_index = lax.broadcasted_iota(jnp.int32, (bin_total, channels, 1), 0)
    inside = (
        (bin_index >= band_low[None, :, None]) & (bin_index < band_high[None, :, None])
    ).astype(jnp.float32)
    shaped = spectrum.reshape(2, bin_total, channels, windows)
    return (
        (shaped / divisor * inside).astype(jnp.bfloat16).reshape(2, bin_total, channels * windows)
    )


def whiten(records, window_valid, band_low, band_high):
    channels, windows, length = records.shape
    bin_total = length // 2
    row_total = channels * windows
    one_bit = (jnp.sign(records.astype(jnp.float32)) * window_valid[:, :, None]).astype(
        jnp.bfloat16
    )
    one_bit = one_bit.reshape(row_total, length)
    blocks = []
    for first_bin in range(0, bin_total, 256):
        dft_block = dft_table(length, first_bin, 256)
        partial_spec = lax.dot_general(
            dft_block, one_bit, (((0,), (1,)), ((), ())), preferred_element_type=jnp.float32
        )
        blocks.append(partial_spec.reshape(2, 256, row_total))
    spectrum = jnp.concatenate(blocks, axis=1)
    return finish(spectrum, band_low, band_high, channels, windows)


def cross_stack(first_spec, second_spec, first_flags, second_flags, in_use):
    real_part = jnp.einsum(
        "fsim,fsjm->sfij", first_spec[0], second_spec[0], preferred_element_type=jnp.float32
    )
    real_part = real_part + jnp.einsum(
        "fsim,fsjm->sfij", first_spec[1], second_spec[1], preferred_element_type=jnp.float32
    )
    imag_part = jnp.einsum(
        "fsim,fsjm->sfij", first_spec[1], second_spec[0], preferred_element_type=jnp.float32
    )
    imag_part = imag_part - jnp.einsum(
        "fsim,fsjm->sfij", first_spec[0], second_spec[1], preferred_element_type=jnp.float32
    )
    common = jnp.einsum("sim,sjm->sij", first_flags, second_flags, precision=lax.Precision.HIGHEST)
    weight = in_use[:, None, None] / jnp.maximum(common, 1.0)
    both = jnp.stack([real_part, imag_part], axis=2) * weight[:, None, None]
    return both.reshape(both.shape[0], both.shape[1], -1).astype(jnp.bfloat16)


def body(records, window_valid, band_low, band_high, pair_counts, partners):
    channels, windows, length = records.shape
    bin_total = length // 2
    readers, slot_count = partners.shape
    bin_share = bin_total // readers
    whitened = whiten(records, window_valid, band_low, band_high)
    arrived = lax.all_to_all(whitened, "chan", split_axis=1, concat_axis=2, tiled=True)
    spectra = arrived.reshape(2, bin_share, readers, channels, windows)
    copies = jnp.broadcast_to(window_valid[None], (readers, channels, windows))
    valid_all = lax.all_to_all(copies, "chan", split_axis=0, concat_axis=0, tiled=True)
    results = []
    for slot_index in range(slot_count):
        partner_ids = partners[:, slot_index]
        picks = partner_ids[:, None] == jnp.arange(readers, dtype=jnp.int32)[None, :]
        partner_spec = jnp.einsum("rq,cfqim->cfrim", picks.astype(jnp.bfloat16), spectra)
        partner_flags = jnp.einsum(
            "rq,qim->rim", picks.astype(jnp.float32), valid_all, precision=lax.Precision.HIGHEST
        )
        in_use = (slot_index < pair_counts).astype(jnp.float32)
        results.append(cross_stack(spectra, partner_spec, valid_all, partner_flags, in_use))
    stacked = jnp.stack(results, axis=1)
    return lax.all_to_all(stacked, "chan", split_axis=0, concat_axis=2, tiled=True)


LANES = 128


def packed_table(length, share, readers):
    bins = np.arange(readers * share).reshape(readers // 2, 2, share)
    samples = np.arange(length)
    phase = (samples[None, :, None, None] * bins[:, None]) % length
    angles = phase.astype(np.float32) * np.float32(2.0 * math.pi / length)
    table = np.stack([np.cos(angles), -np.sin(angles)], axis=3)
    return table.reshape(readers // 2, length, 4 * share).astype(ml_dtypes.bfloat16)


def packed_band(share):
    lane = np.arange(2 * share) % share
    rows = np.arange(3)[:, None] * share - share + lane[None, :]
    near = np.abs(rows[:, :, None] - lane[None, None, :]) <= SMOOTH
    return (near * 0.5).astype(ml_dtypes.bfloat16)


def fused_kernel(
    n,
    bin_total,
    records_in,
    valid_in,
    low_in,
    high_in,
    counts_in,
    partners_in,
    table,
    band_in,
    out,
    records,
    valid,
    low,
    high,
    counts,
    partners,
    band,
    tables,
    raw,
    signs,
    spec,
    mags,
    send,
    recv,
    valids,
    full,
    turned,
    stacked,
    table_sem,
    valid_send,
    valid_recv,
    spec_send,
    spec_recv,
    out_send,
    out_recv,
    own_sem,
    in_sem,
):
    me = lax.axis_index("chan")
    channels, windows, length = records.shape
    share = bin_total // n
    rows = channels * windows
    slots = partners.shape[1]

    half_size = n // 2

    def peer(step, sign=1):
        near = (step - 1) % 2
        shift = (step - 1) // 2 + near
        side = (me // half_size + 1 + near) % 2
        return side * half_size + (me + half_size + sign * shift) % half_size

    barrier = pltpu.get_barrier_semaphore()
    for step in range(1, n):
        pl.semaphore_signal(
            barrier, inc=1, device_id={"chan": peer(step)}, device_id_type=pl.DeviceIdType.MESH
        )

    def table_copy(chunk):
        return pltpu.make_async_copy(table.at[chunk], tables.at[chunk], table_sem.at[chunk])

    inputs = [
        pltpu.make_async_copy(source, target, in_sem.at[i])
        for i, (source, target) in enumerate(
            [
                (records_in, records),
                (valid_in, valid),
                (low_in, low),
                (high_in, high),
                (counts_in, counts),
                (partners_in, partners),
                (band_in, band),
            ]
        )
    ]
    for copy in inputs:
        copy.start()
    for chunk in range(n // 2):
        table_copy(chunk).start()
    for copy in inputs:
        copy.wait()

    valids[me] = valid[...]

    def to_signs(part, _):
        at = pl.multiple_of(part * LANES, LANES)
        raw[...] = records[:, :, pl.ds(at, LANES)].astype(jnp.float32).reshape(rows, LANES)
        for pair in range(windows // 2):
            halves = []
            for window in (2 * pair, 2 * pair + 1):
                x = raw[pl.ds(window, channels, stride=windows), :]
                v = valid[:, window : window + 1]
                halves.append(jnp.where(x > 0, v, jnp.where(x < 0, -v, 0.0)))
            signs[pl.ds(pair * 2 * channels, 2 * channels), pl.ds(at, LANES)] = jnp.concatenate(
                halves, axis=0
            ).astype(jnp.bfloat16)
        return 0

    lax.fori_loop(0, length // LANES, to_signs, 0)

    mags[0] = jnp.zeros((rows, LANES), jnp.bfloat16)
    mags[n + 1] = jnp.zeros((rows, LANES), jnp.bfloat16)

    def transform(chunk, _):
        table_copy(chunk).wait()
        x = jnp.dot(signs[...], tables[chunk], preferred_element_type=jnp.float32)
        for half in range(2):
            y = x[:, half * LANES : (half + 1) * LANES]
            spec[2 * chunk + half] = y
            power = y * y
            mags[2 * chunk + half + 1] = jnp.sqrt(power + pltpu.roll(power, share, 1)).astype(
                jnp.bfloat16
            )
        return 0

    lax.fori_loop(0, n // 2, transform, 0)

    pl.semaphore_wait(barrier, n - 1)

    def valid_copy(source, target):
        return pltpu.make_async_remote_copy(
            src_ref=valids.at[source],
            dst_ref=valids.at[source],
            send_sem=valid_send.at[target],
            recv_sem=valid_recv.at[source],
            device_id={"chan": target},
            device_id_type=pl.DeviceIdType.MESH,
        )

    def spec_copy(source, target):
        return pltpu.make_async_remote_copy(
            src_ref=send.at[target],
            dst_ref=recv.at[source],
            send_sem=spec_send.at[target],
            recv_sem=spec_recv.at[source],
            device_id={"chan": target},
            device_id_type=pl.DeviceIdType.MESH,
        )

    def out_copy(source, target):
        at = pl.multiple_of(source * share, share)
        return pltpu.make_async_remote_copy(
            src_ref=stacked.at[target],
            dst_ref=out.at[:, pl.ds(at, share), :],
            send_sem=out_send.at[target],
            recv_sem=out_recv.at[source],
            device_id={"chan": target},
            device_id_type=pl.DeviceIdType.MESH,
        )

    lane = lax.broadcasted_iota(jnp.int32, (1, LANES), 1)
    first = lane < share
    channel = lax.broadcasted_iota(jnp.int32, (channels, 1), 0)
    lows = jnp.zeros((channels, 1), jnp.int32)
    highs = jnp.zeros((channels, 1), jnp.int32)
    for c in range(channels):
        lows = jnp.where(channel == c, low[c], lows)
        highs = jnp.where(channel == c, high[c], highs)

    def whitened(target):
        total = jnp.dot(mags[target], band[0], preferred_element_type=jnp.float32)
        total += jnp.dot(mags[target + 1], band[1], preferred_element_type=jnp.float32)
        total += jnp.dot(mags[target + 2], band[2], preferred_element_type=jnp.float32)
        k = target * share + jnp.where(first, lane, lane - share)
        near = jnp.minimum(k + SMOOTH, bin_total - 1) - jnp.maximum(k - SMOOTH, 0) + 1
        smoothed = total * (1.0 / near.astype(jnp.float32))
        inside = jnp.where((k >= lows) & (k < highs), 1.0, 0.0)
        y = spec[target] / jnp.maximum(smoothed, 1.0)
        y = y.reshape(windows, channels, LANES) * inside[None]
        return y.reshape(rows, LANES).astype(jnp.bfloat16)

    def send_valid(step, _):
        valid_copy(me, peer(step)).start()
        return 0

    lax.fori_loop(1, n, send_valid, 0)

    def send_spec(step, _):
        target = peer(step)
        send[target] = whitened(target)
        spec_copy(me, target).start()
        return 0

    lax.fori_loop(1, n, send_spec, 0)
    full[me] = whitened(me).astype(jnp.float32)

    def receive(step, _):
        source = peer(step, -1)
        valid_copy(source, me).wait_recv()
        spec_copy(source, me).wait_recv()
        full[source] = recv[source].astype(jnp.float32)
        return 0

    lax.fori_loop(1, n, receive, 0)

    def stack_reader(reader):
        swapped = pltpu.roll(full[reader], share, 1)
        turned[...] = jnp.where(first, swapped, -swapped)
        flags = valids[reader]
        for pair in range(slots // 2):
            ids = [partners[reader, 2 * pair + half] for half in range(2)]

            def window_step(window, totals):
                at = pl.multiple_of(window * channels, channels)
                others = [full[q, pl.ds(at, channels), :] for q in ids]
                totals = list(totals)
                for i in range(channels):
                    straight = full[reader, pl.ds(at + i, 1), :]
                    crossed = turned[pl.ds(at + i, 1), :]
                    for half in range(2):
                        base = half * 2 * channels
                        totals[base + i] += straight * others[half]
                        totals[base + channels + i] += crossed * others[half]
                return tuple(totals)

            zero = jnp.zeros((channels, LANES), jnp.float32)
            totals = lax.fori_loop(
                0, windows, window_step, (zero,) * (4 * channels), unroll=4
            )
            weights = []
            for i in range(channels):
                both = []
                for half in range(2):
                    common = jnp.sum(flags[i : i + 1] * valids[ids[half]], axis=1, keepdims=True)
                    used = jnp.where(2 * pair + half < counts[reader], 1.0, 0.0)
                    both.append(used / jnp.maximum(common, 1.0))
                weights.append(jnp.where(first, both[0], both[1]))
            tiles = []
            for row in range(2 * channels):
                one, two = totals[row], totals[2 * channels + row]
                folded = jnp.where(first, one, two) + pltpu.roll(
                    jnp.where(first, two, one), share, 1
                )
                tiles.append(folded * weights[row % channels])
            flat = jnp.concatenate(tiles, axis=0).T.astype(jnp.bfloat16)
            stacked[reader, 2 * pair] = flat[:share]
            stacked[reader, 2 * pair + 1] = flat[share:]

    def send_stack(step, _):
        reader = peer(step)
        stack_reader(reader)
        out_copy(me, reader).start()
        return 0

    lax.fori_loop(1, n, send_stack, 0)
    stack_reader(me)
    own_at = pl.multiple_of(me * share, share)
    own = pltpu.make_async_copy(stacked.at[me], out.at[:, pl.ds(own_at, share), :], own_sem)
    own.start()
    own.wait()

    def finish_copies(step, _):
        target = peer(step)
        valid_copy(me, target).wait_send()
        spec_copy(me, target).wait_send()
        out_copy(me, target).wait_send()
        out_copy(target, me).wait_recv()
        return 0

    lax.fori_loop(1, n, finish_copies, 0)


def fused(n, records, window_valid, band_low, band_high, pair_counts, partners):
    channels, windows, length = records.shape
    bin_total = length // 2
    slots = partners.shape[1]
    share = bin_total // n
    rows = channels * windows
    table = jnp.asarray(packed_table(length, share, n))
    band = jnp.asarray(packed_band(share))
    hbm = pl.BlockSpec(memory_space=pltpu.HBM)
    dma = pltpu.SemaphoreType.DMA
    out = pl.pallas_call(
        functools.partial(fused_kernel, n, bin_total),
        out_shape=jax.ShapeDtypeStruct((slots, bin_total, LANES), jnp.bfloat16),
        in_specs=[hbm] * 8,
        out_specs=pl.BlockSpec(memory_space=pl.ANY),
        scratch_shapes=[
            pltpu.VMEM(records.shape, jnp.bfloat16),
            pltpu.VMEM(window_valid.shape, jnp.float32),
            pltpu.SMEM(band_low.shape, jnp.int32),
            pltpu.SMEM(band_high.shape, jnp.int32),
            pltpu.SMEM(pair_counts.shape, jnp.int32),
            pltpu.SMEM(partners.shape, jnp.int32),
            pltpu.VMEM(band.shape, jnp.bfloat16),
            pltpu.VMEM(table.shape, jnp.bfloat16),
            pltpu.VMEM((rows, LANES), jnp.float32),
            pltpu.VMEM((rows, length), jnp.bfloat16),
            pltpu.VMEM((n, rows, LANES), jnp.float32),
            pltpu.VMEM((n + 2, rows, LANES), jnp.bfloat16),
            pltpu.VMEM((n, rows, LANES), jnp.bfloat16),
            pltpu.VMEM((n, rows, LANES), jnp.bfloat16),
            pltpu.VMEM((n, channels, windows), jnp.float32),
            pltpu.VMEM((n, rows, LANES), jnp.float32),
            pltpu.VMEM((rows, LANES), jnp.float32),
            pltpu.VMEM((n, slots, share, LANES), jnp.bfloat16),
            dma((n // 2,)),
            dma((n,)),
            dma((n,)),
            dma((n,)),
            dma((n,)),
            dma((n,)),
            dma((n,)),
            dma,
            dma((7,)),
        ],
        compiler_params=pltpu.CompilerParams(
            collective_id=0, has_side_effects=True, vmem_limit_bytes=64 * 1024 * 1024
        ),
    )(records, window_valid, band_low, band_high, pair_counts, partners, table, band)
    return out[None]


def solution(mesh):
    def run(records, window_valid, band_low, band_high, pair_counts, partners):
        n = mesh.shape["chan"]
        channels, windows, length = records.shape
        whole_tiles = 2 * (length // 2 // n) == LANES and 2 * channels * channels == LANES
        args = (records, window_valid, band_low, band_high, pair_counts, partners)
        if whole_tiles and n % 2 == 0 and partners.shape[1] % 2 == 0:
            return fused(n, *args)
        return body(*args)

    return jax.shard_map(
        run,
        mesh=mesh,
        in_specs=(
            P(("groups", "chan"), None, None),
            P(("groups", "chan"), None),
            P(("groups", "chan")),
            P(("groups", "chan")),
            P("groups"),
            P("groups", None),
        ),
        out_specs=P(("groups", "chan"), None, None, None),
        check_vma=False,
    )
```

profile of v0, /device:TPU:0, one launch (start us, length us, event | category | flops | bytes accessed | tf_op | source)
XLA Modules:
  0.0 66.8 jit_solution(17113654329017918036)
XLA Ops:
  0.0 1.4 %copy.9.partners_in = s32[16,4]{1,0:T(8,128)} copy(s32[16,4]{0,1:T(4,128)} %param.13) | data formatting | bytes 512 | tf_op args[5]
  1.4 63.1 %shard_map.82 = bf16[4,1024,128]{2,1,0:T(8,128)(2,1)} custom-call(bf16[8,32,2048]{2,1,0:T(8,128)(2,1)} %records_in.1, f32[8,32]{1,0:T(8,128)} %valid_in.1, s32[8]{0:T(128)} %low_in.1, s32[8]{0:T(128)} %high_in.1, s32[16]{0:T(128)} %counts_in.1, s32[16,4]{1,0:T(8,128)} %copy.9.partners_in, bf16[8,2048,256]{2,1,0:T(8,128)(2,1)} %constant.4.clone.table, ...), custom_call_target="tpu_custom_call" | custom-call | tf_op jit(solution)/shard_map/pallas_call | solution.py:402
  64.5 2.3 %copy.11 = bf16[1,4,1024,128]{3,2,1,0:T(8,128)(2,1)} copy(bf16[1,4,1024,128]{3,2,1,0:T(8,128)(2,1)} %bitcast.1) | data formatting | bytes 2097152
where the time goes:
time: 66.9 us; the launch traced here: 66.8 us
  Pallas kernels  63.1 us (94%)
  local copies, waits for them, and re-layouts  3.62 us (5%)
    pallas_call x1, Pallas kernels, fused(): pl.pallas_call(functools.partial(fused_kernel, n, bin_total), out_shape=j...  63.1 us
    unnamed x2, local copies, waits for them, and re-layouts  3.62 us

commit v1 on v0

--- a/solution.py
+++ b/solution.py
@@ -109,20 +109,53 @@
 LANES = 128
 
 
+def lane_bins(share):
+    lane = np.arange(LANES) % share
+    half = share // 2
+    even_first = 2 * (lane % half) + (lane >= half)
+    odd_first = 2 * (lane % half) + (lane < half)
+    return even_first, odd_first
+
+
 def packed_table(length, share, readers):
-    bins = np.arange(readers * share).reshape(readers // 2, 2, share)
-    samples = np.arange(length)
-    phase = (samples[None, :, None, None] * bins[:, None]) % length
-    angles = phase.astype(np.float32) * np.float32(2.0 * math.pi / length)
-    table = np.stack([np.cos(angles), -np.sin(angles)], axis=3)
-    return table.reshape(readers // 2, length, 4 * share).astype(ml_dtypes.bfloat16)
+    half = share // 2
+    samples = np.arange(length // 2)
+    tables = []
+    for quad in range(readers // 4):
+        for odd in range(2):
+            columns = []
+            for chunk in (2 * quad, 2 * quad + 1):
+                order = (2 * chunk + 1, 2 * chunk) if odd else (2 * chunk, 2 * chunk + 1)
+                bins = np.concatenate([t * share + 2 * np.arange(half) + odd for t in order])
+                phase = (samples[:, None] * bins[None, :]) % length
+                angles = phase.astype(np.float32) * np.float32(2.0 * math.pi / length)
+                columns += [np.cos(angles), -np.sin(angles)]
+            tables.append(np.concatenate(columns, axis=1))
+    return np.stack(tables).reshape(readers // 4, 2, length // 2, 2 * LANES).astype(ml_dtypes.bfloat16)
 
 
 def packed_band(share):
-    lane = np.arange(2 * share) % share
-    rows = np.arange(3)[:, None] * share - share + lane[None, :]
-    near = np.abs(rows[:, :, None] - lane[None, None, :]) <= SMOOTH
-    return (near * 0.5).astype(ml_dtypes.bfloat16)
+    half = share // 2
+    even = 2 * np.arange(half)
+    inner = np.concatenate([even, share + even, share + even + 1, even + 1])
+    rows = np.concatenate([inner - LANES, inner, inner + LANES])
+    even_first, odd_first = lane_bins(share)
+    columns = np.concatenate([even_first, share + odd_first])
+    near = np.abs(rows[:, None] - columns[None, :]) <= SMOOTH
+    return near.astype(ml_dtypes.bfloat16)
+
+
+def packed_fold(share):
+    folds = [np.arange(share)[:, None] == order[None, :] for order in lane_bins(share)]
+    return np.stack([np.concatenate([fold, fold], axis=1) for fold in folds]).astype(
+        ml_dtypes.bfloat16
+    )
+
+
+def packed_spread(channels):
+    lane = np.arange(LANES) % (channels * channels)
+    rows = np.arange(channels)[:, None]
+    return np.stack([rows == lane // channels, rows == lane % channels]).astype(np.float32)
 
 
 def fused_kernel(
@@ -136,6 +169,8 @@
     partners_in,
     table,
     band_in,
+    fold_in,
+    spread_in,
     out,
     records,
     valid,
@@ -144,17 +179,23 @@
     counts,
     partners,
     band,
+    fold,
+    spread,
     tables,
-    raw,
     signs,
     spec,
     mags,
+    moved,
     send,
     recv,
     valids,
+    row_flags,
+    column_flags,
     full,
     turned,
+    compact,
     stacked,
+    state,
     table_sem,
     valid_send,
     valid_recv,
@@ -169,15 +210,16 @@
     channels, windows, length = records.shape
     share = bin_total // n
     rows = channels * windows
-    slots = partners.shape[1]
-
-    half_size = n // 2
-
-    def peer(step, sign=1):
-        near = (step - 1) % 2
-        shift = (step - 1) // 2 + near
-        side = (me // half_size + 1 + near) % 2
-        return side * half_size + (me + half_size + sign * shift) % half_size
+    slots = partners.shape[0]
+    chunks = n // 2
+    quads = n // 4
+    samples = length // 2
+
+    def far_near(count, step):
+        return jnp.where(step % 2 == 0, count // 2 + step // 2, count // 2 - 1 - step // 2)
+
+    def peer(step):
+        return me ^ step
 
     barrier = pltpu.get_barrier_semaphore()
     for step in range(1, n):
@@ -185,64 +227,84 @@
             barrier, inc=1, device_id={"chan": peer(step)}, device_id_type=pl.DeviceIdType.MESH
         )
 
-    def table_copy(chunk):
-        return pltpu.make_async_copy(table.at[chunk], tables.at[chunk], table_sem.at[chunk])
+    def table_copy(quad):
+        return pltpu.make_async_copy(table.at[quad], tables.at[quad], table_sem.at[quad])
 
     inputs = [
         pltpu.make_async_copy(source, target, in_sem.at[i])
         for i, (source, target) in enumerate(
             [
+                (valid_in, valid),
                 (records_in, records),
-                (valid_in, valid),
                 (low_in, low),
                 (high_in, high),
                 (counts_in, counts),
                 (partners_in, partners),
                 (band_in, band),
+                (fold_in, fold),
+                (spread_in, spread),
             ]
         )
     ]
     for copy in inputs:
         copy.start()
-    for chunk in range(n // 2):
-        table_copy(chunk).start()
+    for quad in range(quads):
+        table_copy(quad).start()
     for copy in inputs:
         copy.wait()
 
     valids[me] = valid[...]
 
+    row = lax.broadcasted_iota(jnp.int32, (rows, windows), 0)
+    window_lane = lax.broadcasted_iota(jnp.int32, (rows, windows), 1)
+    spread_valid = jnp.broadcast_to(valid[...][:, None, :], (channels, windows, windows))
+    spread_valid = spread_valid.reshape(rows, windows)
+    level = jnp.sum(
+        jnp.where(row % windows == window_lane, spread_valid, 0.0), axis=1, keepdims=True
+    )
+    level = jnp.broadcast_to(level, (rows, LANES)).astype(jnp.bfloat16)
+
     def to_signs(part, _):
         at = pl.multiple_of(part * LANES, LANES)
-        raw[...] = records[:, :, pl.ds(at, LANES)].astype(jnp.float32).reshape(rows, LANES)
-        for pair in range(windows // 2):
-            halves = []
-            for window in (2 * pair, 2 * pair + 1):
-                x = raw[pl.ds(window, channels, stride=windows), :]
-                v = valid[:, window : window + 1]
-                halves.append(jnp.where(x > 0, v, jnp.where(x < 0, -v, 0.0)))
-            signs[pl.ds(pair * 2 * channels, 2 * channels), pl.ds(at, LANES)] = jnp.concatenate(
-                halves, axis=0
-            ).astype(jnp.bfloat16)
-        return 0
-
-    lax.fori_loop(0, length // LANES, to_signs, 0)
-
-    mags[0] = jnp.zeros((rows, LANES), jnp.bfloat16)
-    mags[n + 1] = jnp.zeros((rows, LANES), jnp.bfloat16)
-
-    def transform(chunk, _):
-        table_copy(chunk).wait()
-        x = jnp.dot(signs[...], tables[chunk], preferred_element_type=jnp.float32)
-        for half in range(2):
-            y = x[:, half * LANES : (half + 1) * LANES]
-            spec[2 * chunk + half] = y
-            power = y * y
-            mags[2 * chunk + half + 1] = jnp.sqrt(power + pltpu.roll(power, share, 1)).astype(
-                jnp.bfloat16
-            )
-        return 0
-
-    lax.fori_loop(0, n // 2, transform, 0)
+        later = pl.multiple_of(samples + part * LANES, LANES)
+
+        def sign(x):
+            one = jnp.ones_like(x)
+            return jnp.where(x > 0, one, jnp.where(x < 0, -one, jnp.zeros_like(x)))
+
+        a = sign(records[:, :, pl.ds(at, LANES)].reshape(rows, LANES))
+        b = sign(records[:, :, pl.ds(later, LANES)].reshape(rows, LANES))
+        signs[0, :, pl.ds(at, LANES)] = (a + b) * level
+        signs[1, :, pl.ds(at, LANES)] = (a - b) * level
+        return 0
+
+    lax.fori_loop(0, samples // LANES, to_signs, 0)
+
+    lane = lax.broadcasted_iota(jnp.int32, (1, LANES), 1)
+    first = lane < share
+    inner = lane % share
+    front = inner < share // 2
+
+    mags[:, 0:LANES] = jnp.zeros((rows, LANES), jnp.bfloat16)
+    mags[:, (chunks + 1) * LANES : (chunks + 2) * LANES] = jnp.zeros((rows, LANES), jnp.bfloat16)
+
+    def transform(quad, _):
+        table_copy(quad).wait()
+        even = jnp.dot(signs[0], tables[quad, 0], preferred_element_type=jnp.float32)
+        odd = jnp.dot(signs[1], tables[quad, 1], preferred_element_type=jnp.float32)
+        for part in range(2):
+            chunk = 2 * quad + part
+            e = even[:, part * LANES : (part + 1) * LANES]
+            o = odd[:, part * LANES : (part + 1) * LANES]
+            spec[2 * chunk] = jnp.where(front, e, o)
+            spec[2 * chunk + 1] = jnp.where(front, o, e)
+            e, o = e * e, o * o
+            e, o = e + pltpu.roll(e, share, 1), o + pltpu.roll(o, share, 1)
+            at = pl.multiple_of((chunk + 1) * LANES, LANES)
+            mags[:, pl.ds(at, LANES)] = jnp.sqrt(jnp.where(first, e, o)).astype(jnp.bfloat16)
+        return 0
+
+    lax.fori_loop(0, quads, transform, 0)
 
     pl.semaphore_wait(barrier, n - 1)
 
@@ -277,8 +339,6 @@
             device_id_type=pl.DeviceIdType.MESH,
         )
 
-    lane = lax.broadcasted_iota(jnp.int32, (1, LANES), 1)
-    first = lane < share
     channel = lax.broadcasted_iota(jnp.int32, (channels, 1), 0)
     lows = jnp.zeros((channels, 1), jnp.int32)
     highs = jnp.zeros((channels, 1), jnp.int32)
@@ -286,17 +346,29 @@
         lows = jnp.where(channel == c, low[c], lows)
         highs = jnp.where(channel == c, high[c], highs)
 
-    def whitened(target):
-        total = jnp.dot(mags[target], band[0], preferred_element_type=jnp.float32)
-        total += jnp.dot(mags[target + 1], band[1], preferred_element_type=jnp.float32)
-        total += jnp.dot(mags[target + 2], band[2], preferred_element_type=jnp.float32)
-        k = target * share + jnp.where(first, lane, lane - share)
-        near = jnp.minimum(k + SMOOTH, bin_total - 1) - jnp.maximum(k - SMOOTH, 0) + 1
-        smoothed = total * (1.0 / near.astype(jnp.float32))
-        inside = jnp.where((k >= lows) & (k < highs), 1.0, 0.0)
-        y = spec[target] / jnp.maximum(smoothed, 1.0)
-        y = y.reshape(windows, channels, LANES) * inside[None]
-        return y.reshape(rows, LANES).astype(jnp.bfloat16)
+    def whiten(chunk):
+        at = pl.multiple_of(chunk * LANES, LANES)
+        total = jnp.dot(
+            mags[:, pl.ds(at, 3 * LANES)], band[...], preferred_element_type=jnp.float32
+        )
+        for part in range(2):
+            target = 2 * chunk + part
+            k = target * share + 2 * (inner % (share // 2))
+            k = k + jnp.where(front, part, 1 - part)
+            near = jnp.minimum(k + SMOOTH, bin_total - 1) - jnp.maximum(k - SMOOTH, 0) + 1
+            smoothed = total[:, part * LANES : (part + 1) * LANES] * (1.0 / near.astype(jnp.float32))
+            inside = jnp.where((k >= lows) & (k < highs), 1.0, 0.0)
+            y = spec[target] / jnp.maximum(smoothed, 1.0)
+            y = y.reshape(channels, windows, LANES) * inside[:, None, :]
+            moved[part] = y.reshape(rows, LANES)
+            for pair in range(windows // 2):
+                both = [
+                    moved[part, pl.ds(w, channels, stride=windows), :]
+                    for w in (2 * pair, 2 * pair + 1)
+                ]
+                send[target, pl.ds(pair * 2 * channels, 2 * channels), :] = jnp.concatenate(
+                    both, axis=0
+                ).astype(jnp.bfloat16)
 
     def send_valid(step, _):
         valid_copy(me, peer(step)).start()
@@ -305,74 +377,125 @@
     lax.fori_loop(1, n, send_valid, 0)
 
     def send_spec(step, _):
-        target = peer(step)
-        send[target] = whitened(target)
-        spec_copy(me, target).start()
-        return 0
-
-    lax.fori_loop(1, n, send_spec, 0)
-    full[me] = whitened(me).astype(jnp.float32)
+        chunk = (me // 2) ^ far_near(chunks, step)
+        whiten(chunk)
+        for part in range(2):
+            target = 2 * chunk + part
+
+            @pl.when(target != me)
+            def _():
+                spec_copy(me, target).start()
+
+        return 0
+
+    lax.fori_loop(0, chunks, send_spec, 0)
+
+    def place(source, block):
+        block = block.astype(jnp.float32)
+        full[source] = block
+        swapped = pltpu.roll(block, share, 1)
+        turned[source] = jnp.where(first, -swapped, swapped)
+
+    def spread_flags(source):
+        flags = valids[source]
+        for which, target in ((0, row_flags), (1, column_flags)):
+            target[source] = lax.dot_general(
+                flags,
+                spread[which],
+                (((0,), (0,)), ((), ())),
+                precision=lax.Precision.HIGHEST,
+                preferred_element_type=jnp.float32,
+            )
+
+    place(me, send[me])
+    spread_flags(me)
+
+    def receive_valid(step, _):
+        source = peer(step)
+        valid_copy(source, me).wait_recv()
+        spread_flags(source)
+        return 0
+
+    lax.fori_loop(1, n, receive_valid, 0)
 
     def receive(step, _):
-        source = peer(step, -1)
-        valid_copy(source, me).wait_recv()
+        source = me ^ far_near(n, step)
         spec_copy(source, me).wait_recv()
-        full[source] = recv[source].astype(jnp.float32)
-        return 0
-
-    lax.fori_loop(1, n, receive, 0)
-
-    def stack_reader(reader):
-        swapped = pltpu.roll(full[reader], share, 1)
-        turned[...] = jnp.where(first, swapped, -swapped)
-        flags = valids[reader]
-        for pair in range(slots // 2):
-            ids = [partners[reader, 2 * pair + half] for half in range(2)]
-
-            def window_step(window, totals):
-                at = pl.multiple_of(window * channels, channels)
-                others = [full[q, pl.ds(at, channels), :] for q in ids]
-                totals = list(totals)
-                for i in range(channels):
-                    straight = full[reader, pl.ds(at + i, 1), :]
-                    crossed = turned[pl.ds(at + i, 1), :]
-                    for half in range(2):
-                        base = half * 2 * channels
-                        totals[base + i] += straight * others[half]
-                        totals[base + channels + i] += crossed * others[half]
-                return tuple(totals)
-
-            zero = jnp.zeros((channels, LANES), jnp.float32)
-            totals = lax.fori_loop(
-                0, windows, window_step, (zero,) * (4 * channels), unroll=4
-            )
-            weights = []
+        place(source, recv[source])
+        return 0
+
+    lax.fori_loop(0, n - 1, receive, 0)
+
+    folding = fold[me % 2]
+
+    def order(place_index):
+        return me ^ far_near(n, place_index)
+
+    def stack_entry(entry):
+        place_index = state[0]
+        slot = state[1]
+        reader = order(place_index % n)
+        partner = partners[slot, reader]
+
+        def window_step(window, totals):
+            at = pl.multiple_of(window * channels, channels)
+            straight = full[partner, pl.ds(at, channels), :]
+            crossed = turned[partner, pl.ds(at, channels), :]
+            totals = list(totals)
             for i in range(channels):
-                both = []
-                for half in range(2):
-                    common = jnp.sum(flags[i : i + 1] * valids[ids[half]], axis=1, keepdims=True)
-                    used = jnp.where(2 * pair + half < counts[reader], 1.0, 0.0)
-                    both.append(used / jnp.maximum(common, 1.0))
-                weights.append(jnp.where(first, both[0], both[1]))
-            tiles = []
-            for row in range(2 * channels):
-                one, two = totals[row], totals[2 * channels + row]
-                folded = jnp.where(first, one, two) + pltpu.roll(
-                    jnp.where(first, two, one), share, 1
-                )
-                tiles.append(folded * weights[row % channels])
-            flat = jnp.concatenate(tiles, axis=0).T.astype(jnp.bfloat16)
-            stacked[reader, 2 * pair] = flat[:share]
-            stacked[reader, 2 * pair + 1] = flat[share:]
-
-    def send_stack(step, _):
-        reader = peer(step)
-        stack_reader(reader)
-        out_copy(me, reader).start()
-        return 0
-
-    lax.fori_loop(1, n, send_stack, 0)
-    stack_reader(me)
+                own = full[reader, pl.ds(at + i, 1), :]
+                totals[i] += own * straight
+                totals[channels + i] += own * crossed
+            return tuple(totals)
+
+        zero = jnp.zeros((channels, LANES), jnp.float32)
+        totals = lax.fori_loop(0, windows, window_step, (zero,) * (2 * channels), unroll=4)
+        tile = jnp.concatenate(totals, axis=0)
+        high_part = tile.astype(jnp.bfloat16)
+        low_part = (tile - high_part.astype(jnp.float32)).astype(jnp.bfloat16)
+        flat = lax.dot_general(
+            folding,
+            jnp.concatenate([high_part, low_part], axis=1),
+            (((1,), (1,)), ((), ())),
+            preferred_element_type=jnp.float32,
+        )
+        common = jnp.sum(row_flags[reader] * column_flags[partner], axis=0, keepdims=True)
+        compact[entry] = (flat * (1.0 / jnp.maximum(common, 1.0))).astype(jnp.bfloat16)
+        more = slot + 1 < counts[reader]
+        state[0] = jnp.where(more, place_index, place_index + 1)
+        state[1] = jnp.where(more, slot + 1, 0)
+
+    entries = 2 * n
+    ready = [min(slots * (p + 1), entries - (n - 1 - p)) for p in range(n)]
+    added = [now - before for now, before in zip(ready, [0] + ready)]
+
+    def send_stack(begin, shift, width, place_index, _):
+        for extra in range(width):
+            stack_entry(begin + (place_index - shift) * width + extra)
+        base = state[2]
+        reader = order(place_index)
+        count = counts[reader]
+        for slot in range(slots):
+            block = compact[jnp.minimum(base + slot, entries - 1)]
+            stacked[reader, slot] = jnp.where(slot < count, block, jnp.zeros_like(block))
+
+        @pl.when(place_index < n - 1)
+        def _():
+            out_copy(me, reader).start()
+
+        state[2] = base + count
+        return 0
+
+    for i in range(3):
+        state[i] = 0
+    p = 0
+    while p < n:
+        stop = p
+        while stop < n and added[stop] == added[p]:
+            stop += 1
+        step = functools.partial(send_stack, ready[p] - added[p], p, added[p])
+        lax.fori_loop(p, stop, step, 0)
+        p = stop
     own_at = pl.multiple_of(me * share, share)
     own = pltpu.make_async_copy(stacked.at[me], out.at[:, pl.ds(own_at, share), :], own_sem)
     own.start()
@@ -397,12 +520,15 @@
     rows = channels * windows
     table = jnp.asarray(packed_table(length, share, n))
     band = jnp.asarray(packed_band(share))
+    fold = jnp.asarray(packed_fold(share))
+    spread = jnp.asarray(packed_spread(channels))
     hbm = pl.BlockSpec(memory_space=pltpu.HBM)
     dma = pltpu.SemaphoreType.DMA
+    by_slot = partners.T
     out = pl.pallas_call(
         functools.partial(fused_kernel, n, bin_total),
         out_shape=jax.ShapeDtypeStruct((slots, bin_total, LANES), jnp.bfloat16),
-        in_specs=[hbm] * 8,
+        in_specs=[hbm] * 10,
         out_specs=pl.BlockSpec(memory_space=pl.ANY),
         scratch_shapes=[
             pltpu.VMEM(records.shape, jnp.bfloat16),
@@ -410,20 +536,26 @@
             pltpu.SMEM(band_low.shape, jnp.int32),
             pltpu.SMEM(band_high.shape, jnp.int32),
             pltpu.SMEM(pair_counts.shape, jnp.int32),
-            pltpu.SMEM(partners.shape, jnp.int32),
+            pltpu.SMEM(by_slot.shape, jnp.int32),
             pltpu.VMEM(band.shape, jnp.bfloat16),
+            pltpu.VMEM(fold.shape, jnp.bfloat16),
+            pltpu.VMEM(spread.shape, jnp.float32),
             pltpu.VMEM(table.shape, jnp.bfloat16),
-            pltpu.VMEM((rows, LANES), jnp.float32),
-            pltpu.VMEM((rows, length), jnp.bfloat16),
+            pltpu.VMEM((2, rows, length // 2), jnp.bfloat16),
             pltpu.VMEM((n, rows, LANES), jnp.float32),
-            pltpu.VMEM((n + 2, rows, LANES), jnp.bfloat16),
+            pltpu.VMEM((rows, (n // 2 + 2) * LANES), jnp.bfloat16),
+            pltpu.VMEM((2, rows, LANES), jnp.float32),
             pltpu.VMEM((n, rows, LANES), jnp.bfloat16),
             pltpu.VMEM((n, rows, LANES), jnp.bfloat16),
             pltpu.VMEM((n, channels, windows), jnp.float32),
+            pltpu.VMEM((n, windows, LANES), jnp.float32),
+            pltpu.VMEM((n, windows, LANES), jnp.float32),
             pltpu.VMEM((n, rows, LANES), jnp.float32),
-            pltpu.VMEM((rows, LANES), jnp.float32),
+            pltpu.VMEM((n, rows, LANES), jnp.float32),
+            pltpu.VMEM((2 * n, share, LANES), jnp.bfloat16),
             pltpu.VMEM((n, slots, share, LANES), jnp.bfloat16),
-            dma((n // 2,)),
+            pltpu.SMEM((3,), jnp.int32),
+            dma((n // 4,)),
             dma((n,)),
             dma((n,)),
             dma((n,)),
@@ -431,12 +563,12 @@
             dma((n,)),
             dma((n,)),
             dma,
-            dma((7,)),
+            dma((9,)),
         ],
         compiler_params=pltpu.CompilerParams(
             collective_id=0, has_side_effects=True, vmem_limit_bytes=64 * 1024 * 1024
         ),
-    )(records, window_valid, band_low, band_high, pair_counts, partners, table, band)
+    )(records, window_valid, band_low, band_high, pair_counts, by_slot, table, band, fold, spread)
     return out[None]
 
 
@@ -446,7 +578,7 @@
         channels, windows, length = records.shape
         whole_tiles = 2 * (length // 2 // n) == LANES and 2 * channels * channels == LANES
         args = (records, window_valid, band_low, band_high, pair_counts, partners)
-        if whole_tiles and n % 2 == 0 and partners.shape[1] % 2 == 0:
+        if whole_tiles and n >= 8 and n & (n - 1) == 0 and windows % 2 == 0:
             return fused(n, *args)
         return body(*args)
 

time: 66.9 us -> 60.5 us (0.904); the launches traced: 66.8 us -> 59.7 us
  Pallas kernels: 63.1 us -> 57.4 us
  local copies, waits for them, and re-layouts: 3.62 us -> 2.26 us
    pallas_call x1, Pallas kernels: 63.1 us -> 57.4 us  [fused(): pl.pallas_call(functools.partial(fused_kernel, n, bin_total), out_shape=j...]
    unnamed x2 -> x1, local copies, waits for them, and re-layouts: 3.62 us -> 2.26 us
where the time goes in v1:
time: 60.5 us; the launch traced here: 59.7 us
  Pallas kernels  57.4 us (95%)
  local copies, waits for them, and re-layouts  2.26 us (4%)
    pallas_call x1, Pallas kernels, fused(): pl.pallas_call(functools.partial(fused_kernel, n, bin_total), out_shape=j...  57.4 us
    unnamed x1, local copies, waits for them, and re-layouts  2.26 us

profile of v1, /device:TPU:0, one launch (start us, length us, event | category | flops | bytes accessed | tf_op | source)
XLA Modules:
  0.0 59.7 jit_solution(15926483635830877416)
XLA Ops:
  0.0 57.4 %shard_map.100 = bf16[4,1024,128]{2,1,0:T(8,128)(2,1)} custom-call(bf16[8,32,2048]{2,1,0:T(8,128)(2,1)} %records_in.1, f32[8,32]{1,0:T(8,128)} %valid_in.1, s32[8]{0:T(128)} %low_in.1, s32[8]{0:T(128)} %high_in.1, s32[16]{0:T(128)} %counts_in.1, s32[4,16]{1,0:T(4,128)} %bitcast.3, bf16[4,2,1024,256]{3,2,1,0:T(8,128)(2,1)} %constant.8.clone.table, ...), custom_call_target="tpu_custom_call" | custom-call | tf_op jit(solution)/shard_map/pallas_call | solution.py:528
  57.4 2.3 %copy.12 = bf16[1,4,1024,128]{3,2,1,0:T(8,128)(2,1)} copy(bf16[1,4,1024,128]{3,2,1,0:T(8,128)(2,1)} %bitcast.2) | data formatting | bytes 2097152

commit v2 on v1

--- a/solution.py
+++ b/solution.py
@@ -155,7 +155,8 @@
 def packed_spread(channels):
     lane = np.arange(LANES) % (channels * channels)
     rows = np.arange(channels)[:, None]
-    return np.stack([rows == lane // channels, rows == lane % channels]).astype(np.float32)
+    both = np.concatenate([rows == lane // channels, rows == lane % channels], axis=1)
+    return np.concatenate([both] * 3).astype(ml_dtypes.bfloat16)
 
 
 def fused_kernel(
@@ -189,8 +190,7 @@
     send,
     recv,
     valids,
-    row_flags,
-    column_flags,
+    flags,
     full,
     turned,
     compact,
@@ -203,7 +203,6 @@
     spec_recv,
     out_send,
     out_recv,
-    own_sem,
     in_sem,
 ):
     me = lax.axis_index("chan")
@@ -360,21 +359,7 @@
             inside = jnp.where((k >= lows) & (k < highs), 1.0, 0.0)
             y = spec[target] / jnp.maximum(smoothed, 1.0)
             y = y.reshape(channels, windows, LANES) * inside[:, None, :]
-            moved[part] = y.reshape(rows, LANES)
-            for pair in range(windows // 2):
-                both = [
-                    moved[part, pl.ds(w, channels, stride=windows), :]
-                    for w in (2 * pair, 2 * pair + 1)
-                ]
-                send[target, pl.ds(pair * 2 * channels, 2 * channels), :] = jnp.concatenate(
-                    both, axis=0
-                ).astype(jnp.bfloat16)
-
-    def send_valid(step, _):
-        valid_copy(me, peer(step)).start()
-        return 0
-
-    lax.fori_loop(1, n, send_valid, 0)
+            send[target] = y.reshape(rows, LANES).astype(jnp.bfloat16)
 
     def send_spec(step, _):
         chunk = (me // 2) ^ far_near(chunks, step)
@@ -385,42 +370,40 @@
             @pl.when(target != me)
             def _():
                 spec_copy(me, target).start()
+                valid_copy(me, target).start()
 
         return 0
 
     lax.fori_loop(0, chunks, send_spec, 0)
 
     def place(source, block):
-        block = block.astype(jnp.float32)
-        full[source] = block
-        swapped = pltpu.roll(block, share, 1)
-        turned[source] = jnp.where(first, -swapped, swapped)
-
-    def spread_flags(source):
-        flags = valids[source]
-        for which, target in ((0, row_flags), (1, column_flags)):
-            target[source] = lax.dot_general(
-                flags,
-                spread[which],
-                (((0,), (0,)), ((), ())),
-                precision=lax.Precision.HIGHEST,
-                preferred_element_type=jnp.float32,
+        moved[...] = block.astype(jnp.float32)
+        for window in range(windows):
+            part = moved[pl.ds(window, channels, stride=windows), :]
+            swapped = pltpu.roll(part, share, 1)
+            full[source, window * channels : (window + 1) * channels] = part
+            turned[source, window * channels : (window + 1) * channels] = jnp.where(
+                first, -swapped, swapped
             )
+        pieces = []
+        rest = valids[source]
+        for _ in range(3):
+            piece = rest.astype(jnp.bfloat16)
+            rest = rest - piece.astype(jnp.float32)
+            pieces.append(piece)
+        flags[source] = lax.dot_general(
+            jnp.concatenate(pieces, axis=0),
+            spread[...],
+            (((0,), (0,)), ((), ())),
+            preferred_element_type=jnp.float32,
+        )
 
     place(me, send[me])
-    spread_flags(me)
-
-    def receive_valid(step, _):
-        source = peer(step)
-        valid_copy(source, me).wait_recv()
-        spread_flags(source)
-        return 0
-
-    lax.fori_loop(1, n, receive_valid, 0)
 
     def receive(step, _):
         source = me ^ far_near(n, step)
         spec_copy(source, me).wait_recv()
+        valid_copy(source, me).wait_recv()
         place(source, recv[source])
         return 0
 
@@ -459,7 +442,8 @@
             (((1,), (1,)), ((), ())),
             preferred_element_type=jnp.float32,
         )
-        common = jnp.sum(row_flags[reader] * column_flags[partner], axis=0, keepdims=True)
+        common = flags[reader, :, 0:LANES] * flags[partner, :, LANES : 2 * LANES]
+        common = jnp.sum(common, axis=0, keepdims=True)
         compact[entry] = (flat * (1.0 / jnp.maximum(common, 1.0))).astype(jnp.bfloat16)
         more = slot + 1 < counts[reader]
         state[0] = jnp.where(more, place_index, place_index + 1)
@@ -497,9 +481,7 @@
         lax.fori_loop(p, stop, step, 0)
         p = stop
     own_at = pl.multiple_of(me * share, share)
-    own = pltpu.make_async_copy(stacked.at[me], out.at[:, pl.ds(own_at, share), :], own_sem)
-    own.start()
-    own.wait()
+    out[:, pl.ds(own_at, share), :] = stacked[me]
 
     def finish_copies(step, _):
         target = peer(step)
@@ -527,9 +509,9 @@
     by_slot = partners.T
     out = pl.pallas_call(
         functools.partial(fused_kernel, n, bin_total),
-        out_shape=jax.ShapeDtypeStruct((slots, bin_total, LANES), jnp.bfloat16),
+        out_shape=pltpu.VMEM((slots, bin_total, LANES), jnp.bfloat16),
         in_specs=[hbm] * 10,
-        out_specs=pl.BlockSpec(memory_space=pl.ANY),
+        out_specs=pl.BlockSpec(memory_space=pltpu.VMEM),
         scratch_shapes=[
             pltpu.VMEM(records.shape, jnp.bfloat16),
             pltpu.VMEM(window_valid.shape, jnp.float32),
@@ -539,17 +521,16 @@
             pltpu.SMEM(by_slot.shape, jnp.int32),
             pltpu.VMEM(band.shape, jnp.bfloat16),
             pltpu.VMEM(fold.shape, jnp.bfloat16),
-            pltpu.VMEM(spread.shape, jnp.float32),
+            pltpu.VMEM(spread.shape, jnp.bfloat16),
             pltpu.VMEM(table.shape, jnp.bfloat16),
             pltpu.VMEM((2, rows, length // 2), jnp.bfloat16),
             pltpu.VMEM((n, rows, LANES), jnp.float32),
             pltpu.VMEM((rows, (n // 2 + 2) * LANES), jnp.bfloat16),
-            pltpu.VMEM((2, rows, LANES), jnp.float32),
+            pltpu.VMEM((rows, LANES), jnp.float32),
             pltpu.VMEM((n, rows, LANES), jnp.bfloat16),
             pltpu.VMEM((n, rows, LANES), jnp.bfloat16),
             pltpu.VMEM((n, channels, windows), jnp.float32),
-            pltpu.VMEM((n, windows, LANES), jnp.float32),
-            pltpu.VMEM((n, windows, LANES), jnp.float32),
+            pltpu.VMEM((n, windows, 2 * LANES), jnp.float32),
             pltpu.VMEM((n, rows, LANES), jnp.float32),
             pltpu.VMEM((n, rows, LANES), jnp.float32),
             pltpu.VMEM((2 * n, share, LANES), jnp.bfloat16),
@@ -562,11 +543,10 @@
             dma((n,)),
             dma((n,)),
             dma((n,)),
-            dma,
             dma((9,)),
         ],
         compiler_params=pltpu.CompilerParams(
-            collective_id=0, has_side_effects=True, vmem_limit_bytes=64 * 1024 * 1024
+            collective_id=0, has_side_effects=True, vmem_limit_bytes=60 * 1024 * 1024
         ),
     )(records, window_valid, band_low, band_high, pair_counts, by_slot, table, band, fold, spread)
     return out[None]

time: 60.5 us -> 58.9 us (0.974)
  local copies, waits for them, and re-layouts: 2.26 us -> 0.97 us
    unnamed x1, local copies, waits for them, and re-layouts: 2.26 us -> 0.97 us
where the time goes in v2:
time: 58.9 us; the launch traced here: 58 us
  Pallas kernels  57 us (97%)
  local copies, waits for them, and re-layouts  0.97 us (2%)
    pallas_call x1, Pallas kernels, fused(): pl.pallas_call(functools.partial(fused_kernel, n, bin_total), out_shape=p...  57 us

profile of v2, /device:TPU:0, one launch (start us, length us, event | category | flops | bytes accessed | tf_op | source)
XLA Modules:
  0.0 58.0 jit_solution(12493391064029511871)
XLA Ops:
  0.0 57.0 %shard_map.100 = bf16[4,1024,128]{2,1,0:T(8,128)(2,1)S(1)} custom-call(bf16[8,32,2048]{2,1,0:T(8,128)(2,1)} %records_in.1, f32[8,32]{1,0:T(8,128)} %valid_in.1, s32[8]{0:T(128)} %low_in.1, s32[8]{0:T(128)} %high_in.1, s32[16]{0:T(128)} %counts_in.1, s32[4,16]{1,0:T(4,128)} %bitcast.3, bf16[4,2,1024,256]{3,2,1,0:T(8,128)(2,1)} %constant.8.clone.table, ...), custom_call_target="tpu_custom_call" | custom-call | tf_op jit(solution)/shard_map/pallas_call | solution.py:510
  57.0 1.0 %copy.12 = bf16[1,4,1024,128]{3,2,1,0:T(8,128)(2,1)} copy(bf16[1,4,1024,128]{3,2,1,0:T(8,128)(2,1)S(1)} %bitcast.2) | data formatting | bytes 2097152

commit v3 on v2

--- a/solution.py
+++ b/solution.py
@@ -110,15 +110,14 @@
 
 
 def lane_bins(share):
-    lane = np.arange(LANES) % share
-    half = share // 2
-    even_first = 2 * (lane % half) + (lane >= half)
-    odd_first = 2 * (lane % half) + (lane < half)
-    return even_first, odd_first
+    quarter = share // 4
+    group = np.arange(LANES) % share // quarter
+    start = group // 2 * 2 * quarter + 2 * (np.arange(LANES) % quarter)
+    return start + group % 2, start + 1 - group % 2
 
 
 def packed_table(length, share, readers):
-    half = share // 2
+    quarter = share // 4
     samples = np.arange(length // 2)
     tables = []
     for quad in range(readers // 4):
@@ -126,7 +125,8 @@
             columns = []
             for chunk in (2 * quad, 2 * quad + 1):
                 order = (2 * chunk + 1, 2 * chunk) if odd else (2 * chunk, 2 * chunk + 1)
-                bins = np.concatenate([t * share + 2 * np.arange(half) + odd for t in order])
+                starts = [t * share + h * share // 2 for h in range(2) for t in order]
+                bins = np.concatenate([start + 2 * np.arange(quarter) + odd for start in starts])
                 phase = (samples[:, None] * bins[None, :]) % length
                 angles = phase.astype(np.float32) * np.float32(2.0 * math.pi / length)
                 columns += [np.cos(angles), -np.sin(angles)]
@@ -135,18 +135,26 @@
 
 
 def packed_band(share):
-    half = share // 2
-    even = 2 * np.arange(half)
-    inner = np.concatenate([even, share + even, share + even + 1, even + 1])
-    rows = np.concatenate([inner - LANES, inner, inner + LANES])
     even_first, odd_first = lane_bins(share)
     columns = np.concatenate([even_first, share + odd_first])
+    front = np.arange(share) // (share // 4) % 2 == 0
+    inner = np.concatenate(
+        [
+            np.where(front, even_first[:share], share + odd_first[:share]),
+            np.where(front, share + odd_first[:share], even_first[:share]),
+        ]
+    )
+    rows = np.concatenate([inner - LANES, inner, inner + LANES])
     near = np.abs(rows[:, None] - columns[None, :]) <= SMOOTH
     return near.astype(ml_dtypes.bfloat16)
 
 
 def packed_fold(share):
-    folds = [np.arange(share)[:, None] == order[None, :] for order in lane_bins(share)]
+    half = share // 2
+    folds = []
+    for order in lane_bins(share):
+        placed = np.tile(order[:half], LANES // half)
+        folds.append(np.arange(half)[:, None] == placed[None, :])
     return np.stack([np.concatenate([fold, fold], axis=1) for fold in folds]).astype(
         ml_dtypes.bfloat16
     )
@@ -213,6 +221,9 @@
     chunks = n // 2
     quads = n // 4
     samples = length // 2
+    half = share // 2
+    packed_windows = windows // 2
+    packed_rows = rows // 2
 
     def far_near(count, step):
         return jnp.where(step % 2 == 0, count // 2 + step // 2, count // 2 - 1 - step // 2)
@@ -247,8 +258,9 @@
     ]
     for copy in inputs:
         copy.start()
-    for quad in range(quads):
-        table_copy(quad).start()
+    half_quads = quads // 2
+    for place in [*range(half_quads, quads), *reversed(range(half_quads))]:
+        table_copy(place + me // (n // 2) * (quads - 1 - 2 * place)).start()
     for copy in inputs:
         copy.wait()
 
@@ -282,12 +294,20 @@
     lane = lax.broadcasted_iota(jnp.int32, (1, LANES), 1)
     first = lane < share
     inner = lane % share
-    front = inner < share // 2
+    quarter = share // 4
+    front = inner // quarter % 2 == 0
+    lower = inner < half
 
     mags[:, 0:LANES] = jnp.zeros((rows, LANES), jnp.bfloat16)
     mags[:, (chunks + 1) * LANES : (chunks + 2) * LANES] = jnp.zeros((rows, LANES), jnp.bfloat16)
 
-    def transform(quad, _):
+    upper = me // (n // 2)
+
+    def mirrored(place, count):
+        return place + upper * (count - 1 - 2 * place)
+
+    def transform(place, _):
+        quad = mirrored(place, quads)
         table_copy(quad).wait()
         even = jnp.dot(signs[0], tables[quad, 0], preferred_element_type=jnp.float32)
         odd = jnp.dot(signs[1], tables[quad, 1], preferred_element_type=jnp.float32)
@@ -303,7 +323,7 @@
             mags[:, pl.ds(at, LANES)] = jnp.sqrt(jnp.where(first, e, o)).astype(jnp.bfloat16)
         return 0
 
-    lax.fori_loop(0, quads, transform, 0)
+    lax.fori_loop(quads // 2, quads, transform, 0)
 
     pl.semaphore_wait(barrier, n - 1)
 
@@ -317,23 +337,23 @@
             device_id_type=pl.DeviceIdType.MESH,
         )
 
-    def spec_copy(source, target):
+    def spec_copy(part, source, target):
         return pltpu.make_async_remote_copy(
-            src_ref=send.at[target],
-            dst_ref=recv.at[source],
-            send_sem=spec_send.at[target],
-            recv_sem=spec_recv.at[source],
+            src_ref=send.at[part, target],
+            dst_ref=recv.at[part, source],
+            send_sem=spec_send.at[part, target],
+            recv_sem=spec_recv.at[part, source],
             device_id={"chan": target},
             device_id_type=pl.DeviceIdType.MESH,
         )
 
-    def out_copy(source, target):
-        at = pl.multiple_of(source * share, share)
+    def out_copy(part, source, target):
+        at = pl.multiple_of(source * share + part * half, half)
         return pltpu.make_async_remote_copy(
-            src_ref=stacked.at[target],
-            dst_ref=out.at[:, pl.ds(at, share), :],
-            send_sem=out_send.at[target],
-            recv_sem=out_recv.at[source],
+            src_ref=stacked.at[part, target],
+            dst_ref=out.at[:, pl.ds(at, half), :],
+            send_sem=out_send.at[part, target],
+            recv_sem=out_recv.at[part, source],
             device_id={"chan": target},
             device_id_type=pl.DeviceIdType.MESH,
         )
@@ -352,39 +372,73 @@
         )
         for part in range(2):
             target = 2 * chunk + part
-            k = target * share + 2 * (inner % (share // 2))
+            k = target * share + inner // half * half + 2 * (inner % quarter)
             k = k + jnp.where(front, part, 1 - part)
             near = jnp.minimum(k + SMOOTH, bin_total - 1) - jnp.maximum(k - SMOOTH, 0) + 1
             smoothed = total[:, part * LANES : (part + 1) * LANES] * (1.0 / near.astype(jnp.float32))
             inside = jnp.where((k >= lows) & (k < highs), 1.0, 0.0)
             y = spec[target] / jnp.maximum(smoothed, 1.0)
             y = y.reshape(channels, windows, LANES) * inside[:, None, :]
-            send[target] = y.reshape(rows, LANES).astype(jnp.bfloat16)
-
-    def send_spec(step, _):
-        chunk = (me // 2) ^ far_near(chunks, step)
+            early = y[:, :packed_windows].reshape(packed_rows, LANES)
+            late = y[:, packed_windows:].reshape(packed_rows, LANES)
+            send[0, target] = jnp.where(lower, early, pltpu.roll(late, half, 1)).astype(
+                jnp.bfloat16
+            )
+            send[1, target] = jnp.where(lower, pltpu.roll(early, LANES - half, 1), late).astype(
+                jnp.bfloat16
+            )
+
+    def send_spec(place):
+        chunk = mirrored(place, chunks)
         whiten(chunk)
         for part in range(2):
             target = 2 * chunk + part
 
             @pl.when(target != me)
             def _():
-                spec_copy(me, target).start()
-                valid_copy(me, target).start()
-
-        return 0
-
-    lax.fori_loop(0, chunks, send_spec, 0)
+                spec_copy(0, me, target).start()
+
+    inside_far = chunks // 2 - 1
+
+    def send_far(step, _):
+        send_spec(chunks // 2 + 1 + (me // 2 + step) % inside_far)
+        return 0
+
+    lax.fori_loop(0, inside_far, send_far, 0)
+
+    def send_rest(step, _):
+        quad = half_quads - 1 - step
+        transform(quad, 0)
+        for c in (2, 1):
+            send_spec(2 * quad + c)
+        return 0
+
+    lax.fori_loop(0, half_quads, send_rest, 0)
+    send_spec(0)
+
+    def send_valid(step, _):
+        valid_copy(me, me ^ far_near(n, step)).start()
+        return 0
+
+    lax.fori_loop(0, n - 1, send_valid, 0)
+
+    def send_later(step, _):
+        spec_copy(1, me, me ^ far_near(n, step)).start()
+        return 0
+
+    lax.fori_loop(0, n - 1, send_later, 0)
 
     def place(source, block):
         moved[...] = block.astype(jnp.float32)
-        for window in range(windows):
-            part = moved[pl.ds(window, channels, stride=windows), :]
+        for window in range(packed_windows):
+            part = moved[pl.ds(window, channels, stride=packed_windows), :]
             swapped = pltpu.roll(part, share, 1)
             full[source, window * channels : (window + 1) * channels] = part
             turned[source, window * channels : (window + 1) * channels] = jnp.where(
                 first, -swapped, swapped
             )
+
+    def spread_flags(source):
         pieces = []
         rest = valids[source]
         for _ in range(3):
@@ -398,16 +452,16 @@
             preferred_element_type=jnp.float32,
         )
 
-    place(me, send[me])
-
-    def receive(step, _):
+    spread_flags(me)
+
+    def receive(part, step, _):
         source = me ^ far_near(n, step)
-        spec_copy(source, me).wait_recv()
-        valid_copy(source, me).wait_recv()
-        place(source, recv[source])
-        return 0
-
-    lax.fori_loop(0, n - 1, receive, 0)
+        spec_copy(part, source, me).wait_recv()
+        if part == 0:
+            valid_copy(source, me).wait_recv()
+            spread_flags(source)
+        place(source, recv[part, source])
+        return 0
 
     folding = fold[me % 2]
 
@@ -432,7 +486,7 @@
             return tuple(totals)
 
         zero = jnp.zeros((channels, LANES), jnp.float32)
-        totals = lax.fori_loop(0, windows, window_step, (zero,) * (2 * channels), unroll=4)
+        totals = lax.fori_loop(0, packed_windows, window_step, (zero,) * (2 * channels), unroll=4)
         tile = jnp.concatenate(totals, axis=0)
         high_part = tile.astype(jnp.bfloat16)
         low_part = (tile - high_part.astype(jnp.float32)).astype(jnp.bfloat16)
@@ -453,7 +507,7 @@
     ready = [min(slots * (p + 1), entries - (n - 1 - p)) for p in range(n)]
     added = [now - before for now, before in zip(ready, [0] + ready)]
 
-    def send_stack(begin, shift, width, place_index, _):
+    def send_stack(part, begin, shift, width, place_index, _):
         for extra in range(width):
             stack_entry(begin + (place_index - shift) * width + extra)
         base = state[2]
@@ -461,34 +515,38 @@
         count = counts[reader]
         for slot in range(slots):
             block = compact[jnp.minimum(base + slot, entries - 1)]
-            stacked[reader, slot] = jnp.where(slot < count, block, jnp.zeros_like(block))
+            stacked[part, reader, slot] = jnp.where(slot < count, block, jnp.zeros_like(block))
 
         @pl.when(place_index < n - 1)
         def _():
-            out_copy(me, reader).start()
+            out_copy(part, me, reader).start()
 
         state[2] = base + count
         return 0
 
-    for i in range(3):
-        state[i] = 0
-    p = 0
-    while p < n:
-        stop = p
-        while stop < n and added[stop] == added[p]:
-            stop += 1
-        step = functools.partial(send_stack, ready[p] - added[p], p, added[p])
-        lax.fori_loop(p, stop, step, 0)
-        p = stop
-    own_at = pl.multiple_of(me * share, share)
-    out[:, pl.ds(own_at, share), :] = stacked[me]
+    for part in range(2):
+        place(me, send[part, me])
+        lax.fori_loop(0, n - 1, functools.partial(receive, part), 0)
+        for i in range(3):
+            state[i] = 0
+        p = 0
+        while p < n:
+            stop = p
+            while stop < n and added[stop] == added[p]:
+                stop += 1
+            step = functools.partial(send_stack, part, ready[p] - added[p], p, added[p])
+            lax.fori_loop(p, stop, step, 0)
+            p = stop
+        own_at = pl.multiple_of(me * share + part * half, half)
+        out[:, pl.ds(own_at, half), :] = stacked[part, me]
 
     def finish_copies(step, _):
         target = peer(step)
         valid_copy(me, target).wait_send()
-        spec_copy(me, target).wait_send()
-        out_copy(me, target).wait_send()
-        out_copy(target, me).wait_recv()
+        for part in range(2):
+            spec_copy(part, me, target).wait_send()
+            out_copy(part, me, target).wait_send()
+            out_copy(part, target, me).wait_recv()
         return 0
 
     lax.fori_loop(1, n, finish_copies, 0)
@@ -526,23 +584,23 @@
             pltpu.VMEM((2, rows, length // 2), jnp.bfloat16),
             pltpu.VMEM((n, rows, LANES), jnp.float32),
             pltpu.VMEM((rows, (n // 2 + 2) * LANES), jnp.bfloat16),
-            pltpu.VMEM((rows, LANES), jnp.float32),
-            pltpu.VMEM((n, rows, LANES), jnp.bfloat16),
-            pltpu.VMEM((n, rows, LANES), jnp.bfloat16),
+            pltpu.VMEM((rows // 2, LANES), jnp.float32),
+            pltpu.VMEM((2, n, rows // 2, LANES), jnp.bfloat16),
+            pltpu.VMEM((2, n, rows // 2, LANES), jnp.bfloat16),
             pltpu.VMEM((n, channels, windows), jnp.float32),
             pltpu.VMEM((n, windows, 2 * LANES), jnp.float32),
-            pltpu.VMEM((n, rows, LANES), jnp.float32),
-            pltpu.VMEM((n, rows, LANES), jnp.float32),
-            pltpu.VMEM((2 * n, share, LANES), jnp.bfloat16),
-            pltpu.VMEM((n, slots, share, LANES), jnp.bfloat16),
+            pltpu.VMEM((n, rows // 2, LANES), jnp.float32),
+            pltpu.VMEM((n, rows // 2, LANES), jnp.float32),
+            pltpu.VMEM((2 * n, share // 2, LANES), jnp.bfloat16),
+            pltpu.VMEM((2, n, slots, share // 2, LANES), jnp.bfloat16),
             pltpu.SMEM((3,), jnp.int32),
             dma((n // 4,)),
             dma((n,)),
             dma((n,)),
-            dma((n,)),
-            dma((n,)),
-            dma((n,)),
-            dma((n,)),
+            dma((2, n)),
+            dma((2, n)),
+            dma((2, n)),
+            dma((2, n)),
             dma((9,)),
         ],
         compiler_params=pltpu.CompilerParams(
@@ -558,7 +616,7 @@
         channels, windows, length = records.shape
         whole_tiles = 2 * (length // 2 // n) == LANES and 2 * channels * channels == LANES
         args = (records, window_valid, band_low, band_high, pair_counts, partners)
-        if whole_tiles and n >= 8 and n & (n - 1) == 0 and windows % 2 == 0:
+        if whole_tiles and n >= 8 and n & (n - 1) == 0 and windows % 32 == 0:
             return fused(n, *args)
         return body(*args)
 

time: 58.9 us -> 56.6 us (0.961)
  Pallas kernels: 57 us -> 55.3 us
    pallas_call x1, Pallas kernels: 57 us -> 55.3 us  [fused(): pl.pallas_call(functools.partial(fused_kernel, n, bin_total), out_shape=p...]
where the time goes in v3:
time: 56.6 us; the launch traced here: 56.2 us
  Pallas kernels  55.3 us (98%)
  local copies, waits for them, and re-layouts  0.97 us (2%)
    pallas_call x1, Pallas kernels, fused(): pl.pallas_call(functools.partial(fused_kernel, n, bin_total), out_shape=p...  55.3 us

profile of v3, /device:TPU:0, one launch (start us, length us, event | category | flops | bytes accessed | tf_op | source)
XLA Modules:
  0.0 56.2 jit_solution(8639773316810550037)
XLA Ops:
  0.0 55.3 %shard_map.100 = bf16[4,1024,128]{2,1,0:T(8,128)(2,1)S(1)} custom-call(bf16[8,32,2048]{2,1,0:T(8,128)(2,1)} %records_in.1, f32[8,32]{1,0:T(8,128)} %valid_in.1, s32[8]{0:T(128)} %low_in.1, s32[8]{0:T(128)} %high_in.1, s32[16]{0:T(128)} %counts_in.1, s32[4,16]{1,0:T(4,128)} %bitcast.3, bf16[4,2,1024,256]{3,2,1,0:T(8,128)(2,1)} %constant.8.clone.table, ...), custom_call_target="tpu_custom_call" | custom-call | tf_op jit(solution)/shard_map/pallas_call | solution.py:568
  55.3 1.0 %copy.12 = bf16[1,4,1024,128]{3,2,1,0:T(8,128)(2,1)} copy(bf16[1,4,1024,128]{3,2,1,0:T(8,128)(2,1)S(1)} %bitcast.2) | data formatting | bytes 2097152

commit v4 on v3

--- a/solution.py
+++ b/solution.py
@@ -107,6 +107,7 @@
 
 
 LANES = 128
+FLAG_ROWS = 16
 
 
 def lane_bins(share):
@@ -164,7 +165,8 @@
     lane = np.arange(LANES) % (channels * channels)
     rows = np.arange(channels)[:, None]
     both = np.concatenate([rows == lane // channels, rows == lane % channels], axis=1)
-    return np.concatenate([both] * 3).astype(ml_dtypes.bfloat16)
+    unused = np.zeros((FLAG_ROWS - channels, 2 * LANES), bool)
+    return np.concatenate([both, unused]).astype(ml_dtypes.bfloat16)
 
 
 def fused_kernel(
@@ -197,7 +199,6 @@
     moved,
     send,
     recv,
-    valids,
     flags,
     full,
     turned,
@@ -205,8 +206,6 @@
     stacked,
     state,
     table_sem,
-    valid_send,
-    valid_recv,
     spec_send,
     spec_recv,
     out_send,
@@ -224,6 +223,7 @@
     half = share // 2
     packed_windows = windows // 2
     packed_rows = rows // 2
+    heights = (packed_rows + FLAG_ROWS, packed_rows)
 
     def far_near(count, step):
         return jnp.where(step % 2 == 0, count // 2 + step // 2, count // 2 - 1 - step // 2)
@@ -232,11 +232,6 @@
         return me ^ step
 
     barrier = pltpu.get_barrier_semaphore()
-    for step in range(1, n):
-        pl.semaphore_signal(
-            barrier, inc=1, device_id={"chan": peer(step)}, device_id_type=pl.DeviceIdType.MESH
-        )
-
     def table_copy(quad):
         return pltpu.make_async_copy(table.at[quad], tables.at[quad], table_sem.at[quad])
 
@@ -258,13 +253,26 @@
     ]
     for copy in inputs:
         copy.start()
-    half_quads = quads // 2
-    for place in [*range(half_quads, quads), *reversed(range(half_quads))]:
+    for place in reversed(range(quads)):
         table_copy(place + me // (n // 2) * (quads - 1 - 2 * place)).start()
+    for step in range(1, n):
+        pl.semaphore_signal(
+            barrier, inc=1, device_id={"chan": peer(step)}, device_id_type=pl.DeviceIdType.MESH
+        )
     for copy in inputs:
         copy.wait()
 
-    valids[me] = valid[...]
+    pieces = []
+    rest = valid[...]
+    for _ in range(3):
+        piece = rest.astype(jnp.bfloat16).astype(jnp.float32)
+        rest = rest - piece
+        pieces.append(piece)
+    unused = jnp.zeros((channels, LANES - 3 * windows), jnp.float32)
+    pieces = jnp.concatenate(pieces + [unused], axis=1)
+    pieces = jnp.concatenate([pieces, jnp.zeros((FLAG_ROWS - channels, LANES), jnp.float32)], axis=0)
+    for target in range(n):
+        send[0, target, rows // 2 : rows // 2 + FLAG_ROWS] = pieces.astype(jnp.bfloat16)
 
     row = lax.broadcasted_iota(jnp.int32, (rows, windows), 0)
     window_lane = lax.broadcasted_iota(jnp.int32, (rows, windows), 1)
@@ -323,24 +331,14 @@
             mags[:, pl.ds(at, LANES)] = jnp.sqrt(jnp.where(first, e, o)).astype(jnp.bfloat16)
         return 0
 
-    lax.fori_loop(quads // 2, quads, transform, 0)
+    transform(quads - 1, 0)
 
     pl.semaphore_wait(barrier, n - 1)
-
-    def valid_copy(source, target):
-        return pltpu.make_async_remote_copy(
-            src_ref=valids.at[source],
-            dst_ref=valids.at[source],
-            send_sem=valid_send.at[target],
-            recv_sem=valid_recv.at[source],
-            device_id={"chan": target},
-            device_id_type=pl.DeviceIdType.MESH,
-        )
 
     def spec_copy(part, source, target):
         return pltpu.make_async_remote_copy(
-            src_ref=send.at[part, target],
-            dst_ref=recv.at[part, source],
+            src_ref=send.at[part, target, pl.ds(0, heights[part])],
+            dst_ref=recv.at[part, source, pl.ds(0, heights[part])],
             send_sem=spec_send.at[part, target],
             recv_sem=spec_recv.at[part, source],
             device_id={"chan": target},
@@ -381,10 +379,10 @@
             y = y.reshape(channels, windows, LANES) * inside[:, None, :]
             early = y[:, :packed_windows].reshape(packed_rows, LANES)
             late = y[:, packed_windows:].reshape(packed_rows, LANES)
-            send[0, target] = jnp.where(lower, early, pltpu.roll(late, half, 1)).astype(
+            send[0, target, 0:packed_rows] = jnp.where(lower, early, pltpu.roll(late, half, 1)).astype(
                 jnp.bfloat16
             )
-            send[1, target] = jnp.where(lower, pltpu.roll(early, LANES - half, 1), late).astype(
+            send[1, target, 0:packed_rows] = jnp.where(lower, pltpu.roll(early, LANES - half, 1), late).astype(
                 jnp.bfloat16
             )
 
@@ -398,29 +396,17 @@
             def _():
                 spec_copy(0, me, target).start()
 
-    inside_far = chunks // 2 - 1
-
-    def send_far(step, _):
-        send_spec(chunks // 2 + 1 + (me // 2 + step) % inside_far)
-        return 0
-
-    lax.fori_loop(0, inside_far, send_far, 0)
+    send_spec(chunks - 1)
 
     def send_rest(step, _):
-        quad = half_quads - 1 - step
+        quad = quads - 2 - step
         transform(quad, 0)
         for c in (2, 1):
             send_spec(2 * quad + c)
         return 0
 
-    lax.fori_loop(0, half_quads, send_rest, 0)
+    lax.fori_loop(0, quads - 1, send_rest, 0)
     send_spec(0)
-
-    def send_valid(step, _):
-        valid_copy(me, me ^ far_near(n, step)).start()
-        return 0
-
-    lax.fori_loop(0, n - 1, send_valid, 0)
 
     def send_later(step, _):
         spec_copy(1, me, me ^ far_near(n, step)).start()
@@ -438,29 +424,23 @@
                 first, -swapped, swapped
             )
 
-    def spread_flags(source):
-        pieces = []
-        rest = valids[source]
-        for _ in range(3):
-            piece = rest.astype(jnp.bfloat16)
-            rest = rest - piece.astype(jnp.float32)
-            pieces.append(piece)
-        flags[source] = lax.dot_general(
-            jnp.concatenate(pieces, axis=0),
-            spread[...],
-            (((0,), (0,)), ((), ())),
-            preferred_element_type=jnp.float32,
-        )
-
-    spread_flags(me)
+    def spread_flags(source, block):
+        spreads = lax.dot_general(
+            block, spread[...], (((0,), (0,)), ((), ())), preferred_element_type=jnp.float32
+        )
+        flags[source] = (
+            spreads[:windows] + spreads[windows : 2 * windows] + spreads[2 * windows : 3 * windows]
+        )
+
+    flag_rows = slice(rows // 2, rows // 2 + FLAG_ROWS)
+    spread_flags(me, send[0, me, flag_rows])
 
     def receive(part, step, _):
         source = me ^ far_near(n, step)
         spec_copy(part, source, me).wait_recv()
         if part == 0:
-            valid_copy(source, me).wait_recv()
-            spread_flags(source)
-        place(source, recv[part, source])
+            spread_flags(source, recv[0, source, flag_rows])
+        place(source, recv[part, source, 0:packed_rows])
         return 0
 
     folding = fold[me % 2]
@@ -525,7 +505,7 @@
         return 0
 
     for part in range(2):
-        place(me, send[part, me])
+        place(me, send[part, me, 0:packed_rows])
         lax.fori_loop(0, n - 1, functools.partial(receive, part), 0)
         for i in range(3):
             state[i] = 0
@@ -540,16 +520,22 @@
         own_at = pl.multiple_of(me * share + part * half, half)
         out[:, pl.ds(own_at, half), :] = stacked[part, me]
 
-    def finish_copies(step, _):
+    def finish_sends(step, _):
         target = peer(step)
-        valid_copy(me, target).wait_send()
         for part in range(2):
             spec_copy(part, me, target).wait_send()
-            out_copy(part, me, target).wait_send()
-            out_copy(part, target, me).wait_recv()
-        return 0
-
-    lax.fori_loop(1, n, finish_copies, 0)
+        out_copy(0, me, target).wait_send()
+        return 0
+
+    def finish_copies(part, step, _):
+        if part == 1:
+            out_copy(1, me, peer(step)).wait_send()
+        out_copy(part, peer(step), me).wait_recv()
+        return 0
+
+    lax.fori_loop(1, n, finish_sends, 0)
+    for part in range(2):
+        lax.fori_loop(1, n, functools.partial(finish_copies, part), 0)
 
 
 def fused(n, records, window_valid, band_low, band_high, pair_counts, partners):
@@ -585,9 +571,8 @@
             pltpu.VMEM((n, rows, LANES), jnp.float32),
             pltpu.VMEM((rows, (n // 2 + 2) * LANES), jnp.bfloat16),
             pltpu.VMEM((rows // 2, LANES), jnp.float32),
-            pltpu.VMEM((2, n, rows // 2, LANES), jnp.bfloat16),
-            pltpu.VMEM((2, n, rows // 2, LANES), jnp.bfloat16),
-            pltpu.VMEM((n, channels, windows), jnp.float32),
+            pltpu.VMEM((2, n, rows // 2 + FLAG_ROWS, LANES), jnp.bfloat16),
+            pltpu.VMEM((2, n, rows // 2 + FLAG_ROWS, LANES), jnp.bfloat16),
             pltpu.VMEM((n, windows, 2 * LANES), jnp.float32),
             pltpu.VMEM((n, rows // 2, LANES), jnp.float32),
             pltpu.VMEM((n, rows // 2, LANES), jnp.float32),
@@ -595,8 +580,6 @@
             pltpu.VMEM((2, n, slots, share // 2, LANES), jnp.bfloat16),
             pltpu.SMEM((3,), jnp.int32),
             dma((n // 4,)),
-            dma((n,)),
-            dma((n,)),
             dma((2, n)),
             dma((2, n)),
             dma((2, n)),
@@ -616,7 +599,7 @@
         channels, windows, length = records.shape
         whole_tiles = 2 * (length // 2 // n) == LANES and 2 * channels * channels == LANES
         args = (records, window_valid, band_low, band_high, pair_counts, partners)
-        if whole_tiles and n >= 8 and n & (n - 1) == 0 and windows % 32 == 0:
+        if whole_tiles and n >= 8 and n & (n - 1) == 0 and windows == 32:
             return fused(n, *args)
         return body(*args)
 

time: 56.6 us -> 55.8 us (0.986)
  Pallas kernels: 55.3 us -> 54.3 us
    pallas_call x1, Pallas kernels: 55.3 us -> 54.3 us  [fused(): pl.pallas_call(functools.partial(fused_kernel, n, bin_total), out_shape=p...]
where the time goes in v4:
time: 55.8 us; the launch traced here: 55.3 us
  Pallas kernels  54.3 us (97%)
  local copies, waits for them, and re-layouts  0.97 us (2%)
    pallas_call x1, Pallas kernels, fused(): pl.pallas_call(functools.partial(fused_kernel, n, bin_total), out_shape=p...  54.3 us

profile of v4, /device:TPU:0, one launch (start us, length us, event | category | flops | bytes accessed | tf_op | source)
XLA Modules:
  0.0 55.3 jit_solution(8470205196943067049)
XLA Ops:
  0.0 54.3 %shard_map.100 = bf16[4,1024,128]{2,1,0:T(8,128)(2,1)S(1)} custom-call(bf16[8,32,2048]{2,1,0:T(8,128)(2,1)} %records_in.1, f32[8,32]{1,0:T(8,128)} %valid_in.1, s32[8]{0:T(128)} %low_in.1, s32[8]{0:T(128)} %high_in.1, s32[16]{0:T(128)} %counts_in.1, s32[4,16]{1,0:T(4,128)} %bitcast.3, bf16[4,2,1024,256]{3,2,1,0:T(8,128)(2,1)} %constant.8.clone.table, ...), custom_call_target="tpu_custom_call" | custom-call | tf_op jit(solution)/shard_map/pallas_call | solution.py:554
  54.3 1.0 %copy.12 = bf16[1,4,1024,128]{3,2,1,0:T(8,128)(2,1)} copy(bf16[1,4,1024,128]{3,2,1,0:T(8,128)(2,1)S(1)} %bitcast.2) | data formatting | bytes 2097152

commit v5 on v4

--- a/solution.py
+++ b/solution.py
@@ -226,7 +226,8 @@
     heights = (packed_rows + FLAG_ROWS, packed_rows)
 
     def far_near(count, step):
-        return jnp.where(step % 2 == 0, count // 2 + step // 2, count // 2 - 1 - step // 2)
+        k = step // 2
+        return jnp.where(step % 2 == 0, count // 2 + (k ^ 2), count // 2 - 1 - k)
 
     def peer(step):
         return me ^ step

time: 55.8 us -> 55.2 us (0.989)
  Pallas kernels: 54.3 us -> 53.6 us
    pallas_call x1, Pallas kernels: 54.3 us -> 53.6 us  [fused(): pl.pallas_call(functools.partial(fused_kernel, n, bin_total), out_shape=p...]
where the time goes in v5:
time: 55.2 us; the launch traced here: 54.6 us
  Pallas kernels  53.6 us (97%)
  local copies, waits for them, and re-layouts  0.97 us (2%)
    pallas_call x1, Pallas kernels, fused(): pl.pallas_call(functools.partial(fused_kernel, n, bin_total), out_shape=p...  53.6 us

profile of v5, /device:TPU:0, one launch (start us, length us, event | category | flops | bytes accessed | tf_op | source)
XLA Modules:
  0.0 54.6 jit_solution(16085548013123387169)
XLA Ops:
  0.0 53.6 %shard_map.100 = bf16[4,1024,128]{2,1,0:T(8,128)(2,1)S(1)} custom-call(bf16[8,32,2048]{2,1,0:T(8,128)(2,1)} %records_in.1, f32[8,32]{1,0:T(8,128)} %valid_in.1, s32[8]{0:T(128)} %low_in.1, s32[8]{0:T(128)} %high_in.1, s32[16]{0:T(128)} %counts_in.1, s32[4,16]{1,0:T(4,128)} %bitcast.3, bf16[4,2,1024,256]{3,2,1,0:T(8,128)(2,1)} %constant.8.clone.table, ...), custom_call_target="tpu_custom_call" | custom-call | tf_op jit(solution)/shard_map/pallas_call | solution.py:555
  53.6 1.0 %copy.12 = bf16[1,4,1024,128]{3,2,1,0:T(8,128)(2,1)} copy(bf16[1,4,1024,128]{3,2,1,0:T(8,128)(2,1)S(1)} %bitcast.2) | data formatting | bytes 2097152

commit v6 on v5

--- a/solution.py
+++ b/solution.py
@@ -260,8 +260,7 @@
         pl.semaphore_signal(
             barrier, inc=1, device_id={"chan": peer(step)}, device_id_type=pl.DeviceIdType.MESH
         )
-    for copy in inputs:
-        copy.wait()
+    inputs[0].wait()
 
     pieces = []
     rest = valid[...]
@@ -284,6 +283,8 @@
     )
     level = jnp.broadcast_to(level, (rows, LANES)).astype(jnp.bfloat16)
 
+    inputs[1].wait()
+
     def to_signs(part, _):
         at = pl.multiple_of(part * LANES, LANES)
         later = pl.multiple_of(samples + part * LANES, LANES)
@@ -299,6 +300,8 @@
         return 0
 
     lax.fori_loop(0, samples // LANES, to_signs, 0)
+    for copy in inputs[2:]:
+        copy.wait()
 
     lane = lax.broadcasted_iota(jnp.int32, (1, LANES), 1)
     first = lane < share
@@ -334,7 +337,6 @@
 
     transform(quads - 1, 0)
 
-    pl.semaphore_wait(barrier, n - 1)
 
     def spec_copy(part, source, target):
         return pltpu.make_async_remote_copy(
@@ -388,8 +390,9 @@
             )
 
     def send_spec(place):
-        chunk = mirrored(place, chunks)
-        whiten(chunk)
+        chunk = mirrored(chunks - 1 if place is None else place, chunks)
+        if place is not None:
+            whiten(chunk)
         for part in range(2):
             target = 2 * chunk + part
 
@@ -397,7 +400,9 @@
             def _():
                 spec_copy(0, me, target).start()
 
-    send_spec(chunks - 1)
+    whiten(mirrored(chunks - 1, chunks))
+    pl.semaphore_wait(barrier, n - 1)
+    send_spec(None)
 
     def send_rest(step, _):
         quad = quads - 2 - step

time: 55.2 us -> 54.5 us (0.987)
  Pallas kernels: 53.6 us -> 52.9 us
    pallas_call x1, Pallas kernels: 53.6 us -> 52.9 us  [fused(): pl.pallas_call(functools.partial(fused_kernel, n, bin_total), out_shape=p...]
where the time goes in v6:
time: 54.5 us; the launch traced here: 53.9 us
  Pallas kernels  52.9 us (97%)
  local copies, waits for them, and re-layouts  0.97 us (2%)
    pallas_call x1, Pallas kernels, fused(): pl.pallas_call(functools.partial(fused_kernel, n, bin_total), out_shape=p...  52.9 us

profile of v6, /device:TPU:0, one launch (start us, length us, event | category | flops | bytes accessed | tf_op | source)
XLA Modules:
  0.0 53.9 jit_solution(1953349680140931675)
XLA Ops:
  0.0 52.9 %shard_map.100 = bf16[4,1024,128]{2,1,0:T(8,128)(2,1)S(1)} custom-call(bf16[8,32,2048]{2,1,0:T(8,128)(2,1)} %records_in.1, f32[8,32]{1,0:T(8,128)} %valid_in.1, s32[8]{0:T(128)} %low_in.1, s32[8]{0:T(128)} %high_in.1, s32[16]{0:T(128)} %counts_in.1, s32[4,16]{1,0:T(4,128)} %bitcast.3, bf16[4,2,1024,256]{3,2,1,0:T(8,128)(2,1)} %constant.8.clone.table, ...), custom_call_target="tpu_custom_call" | custom-call | tf_op jit(solution)/shard_map/pallas_call | solution.py:560
  52.9 1.0 %copy.12 = bf16[1,4,1024,128]{3,2,1,0:T(8,128)(2,1)} copy(bf16[1,4,1024,128]{3,2,1,0:T(8,128)(2,1)S(1)} %bitcast.2) | data formatting | bytes 2097152
